TPU v7x, 32 devices: a whole 2x2x4 slice. The times are simulated.
32 devices in a mesh: grp: 4 (over y, core), dev: 8 (over z, x).
Axes of the slice: x: 2, y: 2, z: 4, core: 2. Of those that a mesh axis runs over, the one named last changes fastest.
Arguments:
- points: bfloat16 [12288, 128], P(('grp', 'dev')), may hold values from -6 to 6
- start_vectors: float32 [12288, 32], P(('grp', 'dev')), may hold values from -6 to 6
Outputs:
- embedding: float32 [12288, 32], P(('grp', 'dev'))
All inputs are finite; a program needn't handle non-finite values.
Results may differ from a plain program's by a relative error of at most 0.005.
Values may be sent and summed in bfloat16 or wider, within the bound.
A program may use at most 128 MiB of HBM per device.

v0:
```python
import math

import jax
import jax.numpy as jnp
from jax import lax
from jax.sharding import PartitionSpec as P

ITERS = 2


sharpness = 8.0
panels_per_block = 16


def unit_rows(points):
    values = points.astype(jnp.float32)
    squares = jnp.sum(values * values, axis=-1, keepdims=True)
    return (values * lax.rsqrt(squares + 1e-06)).astype(jnp.bfloat16)


def tile_weights(own_units, others):
    cosine = lax.dot_general(
        own_units, others, (((1,), (1,)), ((), ())), preferred_element_type=jnp.float32
    )
    return jnp.exp(sharpness * (cosine - 1.0)).astype(jnp.bfloat16)


def weight_panel(own_units, rolled, count):
    tile_rows = own_units.shape[0]
    width = panels_per_block * tile_rows

    def fill(index, panel):
        others = lax.dynamic_slice_in_dim(rolled, index * width, width, 0)
        return lax.dynamic_update_slice_in_dim(
            panel, tile_weights(own_units, others), index * width, 1
        )

    empty = jnp.zeros((tile_rows, count * tile_rows), jnp.bfloat16)
    return lax.fori_loop(0, count // panels_per_block, fill, empty)


def share_iterate(iterate):
    return lax.all_gather(iterate, ("grp", "dev"), axis=0, tiled=True)


def orthonormal(image):
    gram_local = jnp.dot(
        image.T, image, precision=lax.Precision.HIGHEST, preferred_element_type=jnp.float32
    )
    gram_total = lax.psum(gram_local, ("grp", "dev"))
    factor = jnp.linalg.cholesky(gram_total)
    return lax.linalg.triangular_solve(factor, image.T, left_side=True, lower=True).T


def body(points, start_vectors):
    tile_rows = points.shape[0]
    panels = lax.axis_size(("grp", "dev"))
    position = lax.axis_index(("grp", "dev"))
    own_units = unit_rows(points)
    all_units = lax.all_gather(own_units, ("grp", "dev"), axis=0, tiled=True)
    rolled = jnp.roll(all_units, -position * tile_rows, axis=0)
    vectors = start_vectors
    weights = weight_panel(own_units, rolled, panels)
    degree = jnp.sum(weights, axis=1, dtype=jnp.float32)
    scale = lax.rsqrt(degree)[:, None]
    for sweep in range(ITERS):
        iterate = (scale * vectors).astype(jnp.bfloat16)
        gathered = jnp.roll(share_iterate(iterate), -position * tile_rows, axis=0)
        product = jnp.dot(weights, gathered, preferred_element_type=jnp.float32)
        vectors = orthonormal(scale * product)
    return vectors * math.sqrt(tile_rows * panels)


def solution(mesh):
    placed = (P(("grp", "dev"), None), P(("grp", "dev"), None))
    return jax.shard_map(
        body, mesh=mesh, in_specs=placed, out_specs=P(("grp", "dev"), None), check_vma=False
    )
```

profile of v0, /device:TPU:0, one launch (start us, length us, event | category | flops | bytes accessed | tf_op | source)
XLA Modules:
  0.0 339.1 jit_solution(12517805892950426013)
XLA Ops:
  6.5 0.0 all-gather.2.cloned.1.call-start
  6.5 1.0 fusion.12
  7.6 1.7 fusion.13
  9.2 0.0 all-gather.2.cloned.1.call-update
  9.3 62.8 %all-gather.2.cloned.1.call-done = bf16[12288,128]{1,0:T(8,128)(2,1)} async-done(((bf16[384,128]{1,0:T(8,128)(2,1)}), bf16[12288,128]{1,0:T(8,128)(2,1)}) %all-gather.2.cloned.1.call-update) | async-done | bytes 3145744 | tf_op jit(solution)/shard_map/all_gather | solution.py:60
  72.1 4.3 %fusion.4 = bf16[12288,128]{1,0:T(8,128)(2,1)S(1)} fusion(s32[]{:T(128)S(6)} %select_n.35, bf16[12288,128]{1,0:T(8,128)(2,1)} %all-gather.2.cloned.1.call-done), kind=kLoop, calls=%fused_computation.8 | loop fusion | flops 6291456 | bytes 6291460 | tf_op jit(solution)/shard_map/jit(_roll_dynamic)/concatenate | solution.py:61
  76.4 0.0 copy-start.1
  76.4 4.4 %broadcast_in_dim.2 = bf16[384,12288]{0,1:T(8,128)(2,1)} broadcast(bf16[]{:T(256)} %constant.130.clone.1), dimensions={} | broadcast | bytes 9437186 | tf_op jit(solution)/shard_map/broadcast_in_dim | solution.py:38
  80.8 7.7 %while.15 = (s32[]{:T(128)}, bf16[384,12288]{0,1:T(8,128)(2,1)}, bf16[12288,128]{1,0:T(8,128)(2,1)S(1)}, bf16[384,128]{1,0:T(8,128)(2,1)S(1)}, s32[]{:T(128)}, /*index=5*/s32[]{:T(128)}, s32[]{:T(128)}, s32[]{:T(128)}) while((s32[]{:T(128)}, bf16[384,12288]{0,1:T(8,128)(2,1)}, bf16[12288,128]{1,0:T(8,128)(2,1)S(1)}, ...), condition=%wide.region_2.3_spmd, body=%wide.region_1.2_spmd.sunk | while | flops 611057664 | bytes 6390915 | solution.py:39
  80.8 3.8 %fusion.42 = bf16[384,12288]{0,1:T(8,128)(2,1)} fusion(bf16[384,12288]{0,1:T(8,128)(2,1)} %get-tuple-element.161, s32[]{:T(128)S(6)} %select_n.52, bf16[384,128]{1,0:T(8,128)(2,1)S(1)} %get-tuple-element.171, bf16[12288,128]{1,0:T(8,128)(2,1)S(1)} %get-tuple-element.170), kind=kOutput, calls=%fused_computation.2.clone.1 | convolution fusion | flops 611057664 | bytes 6390784 | tf_op jit(solution)/shard_map/while/body/eval_jaxpr/dot_general | solution.py:22
  84.7 3.9 %fusion.42 = bf16[384,12288]{0,1:T(8,128)(2,1)} fusion(bf16[384,12288]{0,1:T(8,128)(2,1)} %get-tuple-element.161, s32[]{:T(128)S(6)} %select_n.52, bf16[384,128]{1,0:T(8,128)(2,1)S(1)} %get-tuple-element.171, bf16[12288,128]{1,0:T(8,128)(2,1)S(1)} %get-tuple-element.170), kind=kOutput, calls=%fused_computation.2.clone.1 | convolution fusion | flops 611057664 | bytes 6390784 | tf_op jit(solution)/shard_map/while/body/eval_jaxpr/dot_general | solution.py:22
  88.5 6.4 %convert_reduce_fusion = f32[384]{0:T(512)S(1)} fusion(bf16[384,12288]{0,1:T(8,128)(2,1)} %get-tuple-element.118), kind=kLoop, calls=%fused_computation.5 | loop fusion | flops 9436800 | bytes 9438720 | tf_op jit(solution)/shard_map/reduce_sum | solution.py:64
  95.0 70.7 %all_gather.10 = bf16[12288,32]{0,1:T(8,128)(2,1)S(1)} all-gather(bf16[384,32]{0,1:T(8,128)(2,1)S(1)} %multiply_convert_fusion), channel_id=1, replica_groups=mesh['grp'=4,'dev'=8] {'grp','dev'}, dimensions={0}, use_global_device_ids=true | all-gather | bytes 811008 | tf_op jit(solution)/shard_map/all_gather | solution.py:43
  165.7 1.7 convolution_multiply_fusion.1
  167.4 0.2 fusion.28
  167.6 37.0 %psum.14 = f32[32,32]{0,1:T(8,128)S(1)} all-reduce(f32[32,32]{0,1:T(8,128)S(1)} %fusion.28), channel_id=1, replica_groups=mesh['grp'=4,'dev'=8] {'grp','dev'}, use_global_device_ids=true, to_apply=%region_4.6 | all-reduce | flops 1024 | bytes 8192 | tf_op jit(solution)/shard_map/psum | solution.py:50
  204.6 0.1 copy.4
  204.7 2.9 cholesky.44
  207.7 0.6 compare_reduce_fusion.1
  208.3 0.7 fusion.16
  209.0 2.4 custom-call.6
  211.4 0.3 fusion.7
  211.7 70.3 %all_gather.11 = bf16[12288,32]{0,1:T(8,128)(2,1)S(1)} all-gather(bf16[384,32]{0,1:T(8,128)(2,1)S(1)} %fusion.7), channel_id=1, replica_groups=mesh['grp'=4,'dev'=8] {'grp','dev'}, dimensions={0}, use_global_device_ids=true | all-gather | bytes 811008 | tf_op jit(solution)/shard_map/all_gather | solution.py:43
  281.9 5.4 %convolution_multiply_fusion = f32[384,32]{0,1:T(8,128)S(1)} fusion(bf16[384,12288]{0,1:T(8,128)(2,1)} %get-tuple-element.118, s32[]{:T(128)S(6)} %select_n.35, bf16[12288,32]{0,1:T(8,128)(2,1)S(1)} %all_gather.11, f32[384]{0:T(512)S(1)} %rsqrt.16), kind=kOutput, calls=%fused_computation.13 | convolution fusion | flops 303575040 | bytes 10274308 | tf_op jit(solution)/shard_map/dot_general | solution.py:69
  287.3 0.2 fusion.29
  287.5 37.1 %psum.15 = f32[32,32]{0,1:T(8,128)S(1)} all-reduce(f32[32,32]{0,1:T(8,128)S(1)} %fusion.29), channel_id=1, replica_groups=mesh['grp'=4,'dev'=8] {'grp','dev'}, use_global_device_ids=true, to_apply=%region_7.11 | all-reduce | flops 1024 | bytes 8192 | tf_op jit(solution)/shard_map/psum | solution.py:50
  324.6 0.1 copy.6
  324.7 2.9 cholesky.55
  327.6 0.6 compare_reduce_fusion
  328.3 0.7 fusion.17
  329.0 2.4 custom-call.7
  331.4 0.9 fusion.5
  (12 shorter events, 0.1 us)
Async XLA Ops:
  6.5 65.6 %all-gather.2.cloned.1.call-start = ((), (), s32[]{:S(2)}) async-start(), calls=%async_computation | async-start | bytes 3244032 | tf_op jit(solution)/shard_map/all_gather | solution.py:60
  76.4 4.4 %copy-start.1 = (bf16[384,128]{1,0:T(8,128)(2,1)S(1)}, bf16[384,128]{1,0:T(8,128)(2,1)}, u32[]{:S(2)}) copy-start(bf16[384,128]{1,0:T(8,128)(2,1)} %fusion.13) | copy-start | bytes 294916
  80.8 14.1 %copy-start.2 = (f32[384,32]{0,1:T(8,128)S(1)}, f32[384,32]{0,1:T(8,128)}, u32[]{:S(2)}) copy-start(f32[384,32]{0,1:T(8,128)} %param.10) | copy-start | bytes 147460
  88.5 77.1 %copy-start = (bf16[384,12288]{0,1:T(8,128)(2,1)S(1)}, bf16[384,12288]{0,1:T(8,128)(2,1)}, u32[]{:S(2)}) copy-start(bf16[384,12288]{0,1:T(8,128)(2,1)} %get-tuple-element.118) | copy-start | bytes 28311556
Sparse Core Ops, SparseCore 0:
  10.3 61.7 all-gather.1
where the time goes:
time: 341 us; the launch traced here: 339 us
  blocking collectives  215 us (63%)
  waiting for transfers between devices  62.9 us (18%)
  other arithmetic  26.8 us (8%)
  matrix products  16.3 us (5%)
  between operations  13.5 us (4%)
  local copies, waits for them, and re-layouts  4.56 us (1%)
    all_gather x2, blocking collectives, share_iterate(): return lax.all_gather(iterate, ('grp', 'dev'), axis=0, tiled=True)  141 us
    psum x2, blocking collectives, orthonormal(): gram_total = lax.psum(gram_local, ('grp', 'dev'))  74.1 us
    all_gather x1, waiting for transfers between devices, body(): all_units = lax.all_gather(own_units, ('grp', 'dev'), axis=0, tiled=True)  62.8 us
    dot_general x2, matrix products, tile_weights(): lax.dot_general(own_units, others, (((1,), (1,)), ((), ())), preferred_el...  7.7 us
    another operation x6, other arithmetic, orthonormal(): factor = jnp.linalg.cholesky(gram_total)  7.19 us
    dot_general x2, matrix products, body(): product = jnp.dot(weights, gathered, preferred_element_type=jnp.float32)  7.1 us
  transfers between devices with their start and end apart: 1, of which 1 were waited for; matrix products, arithmetic and copies ran while one was open for 0% of the time, Pallas kernels for 0%

commit v1 on v0

v1 whole, which is shorter than its diff:
```python
import functools
import math

import jax
import jax.numpy as jnp
from jax import lax
from jax.experimental import pallas as pl
from jax.experimental.pallas import tpu as pltpu
from jax.sharding import PartitionSpec as P

MESH = pl.DeviceIdType.MESH
HIGHEST = lax.Precision.HIGHEST
SLOPE = 8.0 / math.log(2.0)
CHUNK = 128


def layout(grp, dev):
    cores = 2
    deep = 4 if dev % 4 == 0 else dev
    return grp // cores, dev // deep, deep


def kernel(Y, X, Z, pts, start, out, units, it0, it1, weights, plane_buf, line_buf,
           send, zsend, recv, gsend, grecv, lsend, lrecv):
    n = Y * X * Z
    rows = pts.shape[0]
    width = start.shape[1]
    total = 2 * n * rows
    grp = lax.axis_index("grp")
    dev = lax.axis_index("dev")
    y, c = grp // 2, grp % 2
    z, x = dev // X, dev % X

    def device(dy=0, dx=0, dz=0, dc=0):
        return (
            ((y + Y - dy) % Y) * 2 + (c + dc) % 2,
            ((z + Z - dz) % Z) * X + (x + X - dx) % X,
        )

    plane = [(a, b, d) for a in range(Y) for b in range(X) for d in range(2)][1:]

    def slot(dy, dx, dz):
        return (dy * X + dx) * Z + dz

    def view(buf, index, part):
        if part is None:
            return buf.at[index]
        half = buf.shape[1] // 2
        return buf.at[index, pl.ds(part * half, half)]

    def copy(g, buf, src, dst, part, ssem, rsem, target):
        return pltpu.make_async_remote_copy(
            src_ref=view(buf, src, part), dst_ref=view(buf, dst, part),
            send_sem=ssem, recv_sem=recv.at[g, rsem],
            device_id=target, device_id_type=MESH,
        )

    def zcopies(g, buf):
        return [
            copy(g, buf, 0, slot(0, 0, e), None, zsend.at[g, e], slot(0, 0, e), device(dz=e))
            for e in range(1, Z)
        ]

    def forwards(g, buf, dy, dx, dz):
        s = slot(dy, dx, dz)
        plan = []
        if dy == 0 and dx == 0:
            plan += [(slot(0, e, dz), None, slot(0, e, dz), device(dx=e)) for e in range(1, X)]
            plan += [(slot(e, 0, dz), None, slot(e, 0, dz), device(dy=e)) for e in range(1, Y)]
        elif dy == 0:
            plan += [(slot(e, dx, dz), 1, n + slot(e, dx, dz), device(dy=e)) for e in range(1, Y)]
        elif dx == 0:
            plan += [(slot(dy, e, dz), 0, slot(dy, e, dz), device(dx=e)) for e in range(1, X)]
        plan.append((n + s, None, 2 * n + s, device(dc=1)))
        return [
            copy(g, buf, s, dst, part, send.at[g, s, k], rsem, target)
            for k, (dst, part, rsem, target) in enumerate(plan)
        ]

    def arrived(g, buf, index, part, rsem):
        copy(g, buf, index, index, part, zsend.at[g, 0], rsem, device(dc=1)).wait_recv()

    def start_all(copies):
        for one in copies:
            one.start()

    xs = [(0, e) for e in range(1, X)]
    ys = [(e, 0) for e in range(1, Y)]
    diagonal = [(a, b) for a in range(1, Y) for b in range(1, X)]

    def launch(g, buf):
        start_all(zcopies(g, buf))
        start_all(forwards(g, buf, 0, 0, 0))

    def collect(g, buf, visit, carry, first=None, second=None):
        def sibling(dy, dx, dz, carry):
            s = slot(dy, dx, dz)
            arrived(g, buf, n + s, None, 2 * n + s)
            return visit(n + s, carry)

        def column(dz, carry):
            arrived(g, buf, slot(0, 0, dz), None, slot(0, 0, dz))
            start_all(forwards(g, buf, 0, 0, dz))
            return visit(slot(0, 0, dz), carry)

        def sides(dz, carry):
            for dy, dx in xs + ys:
                s = slot(dy, dx, dz)
                arrived(g, buf, s, None, s)
                start_all(forwards(g, buf, dy, dx, dz))
                carry = visit(s, carry)
            return sibling(0, 0, dz, carry)

        def corners(dz, carry):
            for dy, dx in diagonal:
                s = slot(dy, dx, dz)
                arrived(g, buf, s, 0, s)
                arrived(g, buf, s, 1, n + s)
                start_all(forwards(g, buf, dy, dx, dz))
                carry = visit(s, carry)
            for dy, dx in xs + ys:
                carry = sibling(dy, dx, dz, carry)
            return carry

        def rest(dz, carry):
            for dy, dx in diagonal:
                carry = sibling(dy, dx, dz, carry)
            return carry

        carry = visit(0, carry)
        carry = lax.fori_loop(1, Z, column, carry)
        if first is not None:
            first()
        carry = lax.fori_loop(0, Z, sides, carry)
        extra = second() if second is not None else None
        carry = lax.fori_loop(0, Z, corners, carry)
        carry = lax.fori_loop(0, Z, rest, carry)
        return carry, extra

    def finish(g, buf):
        for one in zcopies(g, buf):
            one.wait_send()

        def each(dz, carry):
            for dy, dx in [(0, 0)] + xs + ys + diagonal:
                for one in forwards(g, buf, dy, dx, dz):
                    one.wait_send()
            return carry

        lax.fori_loop(0, Z, each, 0)

    def plane_copies(g):
        return [
            pltpu.make_async_remote_copy(
                src_ref=plane_buf.at[g, 0], dst_ref=plane_buf.at[g, k],
                send_sem=gsend.at[g, k], recv_sem=grecv.at[g, k],
                device_id=device(dy=a, dx=b, dc=d), device_id_type=MESH,
            )
            for k, (a, b, d) in enumerate(plane, 1)
        ]

    def line_copies(g):
        return [
            pltpu.make_async_remote_copy(
                src_ref=line_buf.at[g, 0], dst_ref=line_buf.at[g, e],
                send_sem=lsend.at[g, e], recv_sem=lrecv.at[g, e],
                device_id=device(dz=e), device_id_type=MESH,
            )
            for e in range(1, Z)
        ]

    def gram_start(g, image):
        wide = jnp.concatenate([image, jnp.zeros((128 - width, rows), jnp.float32)], axis=0)
        gram = lax.dot_general(
            image, wide, (((1,), (1,)), ((), ())), precision=HIGHEST,
            preferred_element_type=jnp.float32,
        )
        packed = gram[0:8]
        for k in range(1, width // 8):
            packed = packed + pltpu.roll(gram[8 * k:8 * k + 8], width * k, 1)
        plane_buf[g, 0] = packed
        start_all(plane_copies(g))

    def gram_middle(g):
        for one in plane_copies(g):
            one.wait_recv()
        line_buf[g, 0] = jnp.sum(plane_buf[g], axis=0)
        start_all(line_copies(g))

    def gram_end(g):
        for one in line_copies(g):
            one.wait_recv()
        packed = jnp.sum(line_buf[g], axis=0)
        lane = lax.broadcasted_iota(jnp.int32, (width, 128), 1)
        row = lax.broadcasted_iota(jnp.int32, (width, 128), 0)
        parts = [
            packed if k == 1 else pltpu.roll(packed, (width - width * k) % 128, 1)
            for k in range(width // 8)
        ]
        gram = jnp.concatenate(parts, axis=0)
        table = jnp.where((lane >= width) & (lane < 2 * width), gram, 0.0)
        table = jnp.where(lane == row, 1.0, table)
        row1 = lax.broadcasted_iota(jnp.int32, (width, 1), 0)
        for j in range(width):
            column = table[:, width + j:width + j + 1]
            inverse = 1.0 / column[j:j + 1]
            factor = jnp.where(row1 > j, column * inverse, 0.0)
            table = table - factor * table[j:j + 1]
        pivots = jnp.sum(jnp.where(lane == row + width, table, 0.0), axis=1, keepdims=True)
        return (table * lax.rsqrt(pivots))[:, :width]

    partners = [device(dy=a, dx=b, dc=d) for a, b, d in plane]
    partners += [device(dz=e) for e in range(1, Z)]
    barrier = pltpu.get_barrier_semaphore()
    for partner in partners:
        pl.semaphore_signal(barrier, inc=1, device_id=partner, device_id_type=MESH)

    values = pts[...].astype(jnp.float32)
    squares = jnp.sum(values * values, axis=-1, keepdims=True)
    units[0] = (values * lax.rsqrt(squares + 1e-06)).astype(jnp.bfloat16)
    pl.semaphore_wait(barrier, len(partners))
    launch(0, units)

    def weigh(index, degree):
        own = units[0]
        for k in range(rows // CHUNK):
            piece = pl.ds(k * CHUNK, CHUNK)
            cosine = lax.dot_general(
                units[index, piece], own, (((1,), (1,)), ((), ())),
                preferred_element_type=jnp.float32,
            )
            weight = jnp.exp2(cosine * SLOPE - SLOPE).astype(jnp.bfloat16)
            weights[index, piece] = weight
            weight = weight.astype(jnp.float32)
            degree = degree + jnp.sum(weight.reshape(CHUNK // 8, 8, rows), axis=0)
        return degree

    degree, _ = collect(0, units, weigh, jnp.zeros((8, rows), jnp.float32))
    scale = lax.rsqrt(jnp.sum(degree, axis=0, keepdims=True))

    def times(buf):
        def visit(index, carry):
            return carry + jnp.dot(
                buf[index], weights[index], preferred_element_type=jnp.float32
            )
        return visit

    it0[0] = (scale * start[...].T).astype(jnp.bfloat16)
    launch(1, it0)
    product, _ = collect(1, it0, times(it0), jnp.zeros((width, rows), jnp.float32))
    image = scale * product

    iterate = scale * image
    high = iterate.astype(jnp.bfloat16)
    it1[0, :width] = high
    it1[0, width:] = (iterate - high.astype(jnp.float32)).astype(jnp.bfloat16)
    launch(2, it1)
    gram_start(0, image)
    product, inverse = collect(
        2, it1, times(it1), jnp.zeros((2 * width, rows), jnp.float32),
        first=lambda: gram_middle(0), second=lambda: gram_end(0),
    )
    product = scale * (product[:width] + product[width:])
    image = jnp.dot(inverse, product, precision=HIGHEST, preferred_element_type=jnp.float32)

    gram_start(1, image)
    gram_middle(1)
    inverse = gram_end(1)
    vectors = jnp.dot(inverse, image, precision=HIGHEST, preferred_element_type=jnp.float32)
    out[...] = (vectors * math.sqrt(total)).T

    for g, buf in enumerate((units, it0, it1)):
        finish(g, buf)
    for g in range(2):
        for one in plane_copies(g) + line_copies(g):
            one.wait_send()


def body(points, start_vectors):
    rows, features = points.shape
    width = start_vectors.shape[1]
    Y, X, Z = layout(lax.axis_size("grp"), lax.axis_size("dev"))
    n = Y * X * Z
    slots = 2 * n
    shapes = [
        pltpu.VMEM((slots, rows, features), jnp.bfloat16),
        pltpu.VMEM((slots, width, rows), jnp.bfloat16),
        pltpu.VMEM((slots, 2 * width, rows), jnp.bfloat16),
        pltpu.VMEM((slots, rows, rows), jnp.bfloat16),
        pltpu.VMEM((2, 2 * X * Y, 8, 128), jnp.float32),
        pltpu.VMEM((2, Z, 8, 128), jnp.float32),
        pltpu.SemaphoreType.DMA((3, n, X + Y - 1)),
        pltpu.SemaphoreType.DMA((3, Z)),
        pltpu.SemaphoreType.DMA((3, 3 * n)),
        pltpu.SemaphoreType.DMA((2, 2 * X * Y)),
        pltpu.SemaphoreType.DMA((2, 2 * X * Y)),
        pltpu.SemaphoreType.DMA((2, Z)),
        pltpu.SemaphoreType.DMA((2, Z)),
    ]
    held = slots * rows * 2 * (features + 3 * width + rows)
    return pl.pallas_call(
        functools.partial(kernel, Y, X, Z),
        out_shape=jax.ShapeDtypeStruct((rows, width), jnp.float32),
        in_specs=[pl.BlockSpec(memory_space=pltpu.VMEM)] * 2,
        out_specs=pl.BlockSpec(memory_space=pltpu.VMEM),
        scratch_shapes=shapes,
        compiler_params=pltpu.CompilerParams(
            collective_id=0, has_side_effects=True, vmem_limit_bytes=held + (5 << 20)
        ),
    )(points, start_vectors)


def solution(mesh):
    placed = (P(("grp", "dev"), None), P(("grp", "dev"), None))
    return jax.shard_map(
        body, mesh=mesh, in_specs=placed, out_specs=P(("grp", "dev"), None), check_vma=False
    )
```

time: 341 us -> 70.7 us (0.21)
  blocking collectives: 215 us -> 0 us
  Pallas kernels: 0 us -> 68.8 us
  waiting for transfers between devices: 62.9 us -> 0 us
  other arithmetic: 26.8 us -> 0 us
  matrix products: 16.3 us -> 0 us
  between operations: 13.5 us -> 0.03 us
    all_gather x2 -> x0, blocking collectives: 141 us -> none  [share_iterate(): return lax.all_gather(iterate, ('grp', 'dev'), axis=0, tiled=True)]
    psum x2 -> x0, blocking collectives: 74.1 us -> none  [orthonormal(): gram_total = lax.psum(gram_local, ('grp', 'dev'))]
    pallas_call x0 -> x1, Pallas kernels: none -> 68.8 us  [body(): pl.pallas_call(functools.partial(kernel, Y, X, Z), out_shape=jax.ShapeDty...]
    all_gather x1 -> x0, waiting for transfers between devices: 62.8 us -> none  [body(): all_units = lax.all_gather(own_units, ('grp', 'dev'), axis=0, tiled=True)]
    dot_general x6 -> x0, matrix products: 15.2 us -> none  [the longest x2 7.7 us: tile_weights(): lax.dot_general(own_units, others, (((1,), (1,)), ((), ())), preferred_el...]
    another operation x10 -> x0, other arithmetic: 13.4 us -> none  [the longest x6 7.19 us: orthonormal(): factor = jnp.linalg.cholesky(gram_total)]
    reduce_sum x2 -> x0, other arithmetic: 7.47 us -> none  [the longest x1 6.43 us: body(): degree = jnp.sum(weights, axis=1, dtype=jnp.float32)]
    broadcast_in_dim x1 -> x0, local copies, waits for them, and re-layouts: 4.4 us -> none  [weight_panel(): empty = jnp.zeros((tile_rows, count * tile_rows), jnp.bfloat16)]
  transfers between devices with their start and end apart: 1 -> 0, of which waited for: 1 -> 0; matrix products, arithmetic and copies ran while one was open for 0% -> 0% of each run, Pallas kernels for 0% -> 0%
where the time goes in v1:
time: 70.7 us; the launch traced here: 70.5 us
  Pallas kernels  68.8 us (97%)
  local copies, waits for them, and re-layouts  1.69 us (2%)
    pallas_call x1, Pallas kernels, body(): pl.pallas_call(functools.partial(kernel, Y, X, Z), out_shape=jax.ShapeDty...  68.8 us

profile of v1, /device:TPU:0, one launch (start us, length us, event | category | flops | bytes accessed | tf_op | source)
XLA Modules:
  0.0 70.5 jit_solution(11344673669448535251)
XLA Ops:
  0.0 0.0 copy-start
  0.0 1.0 %copy.3.start = f32[384,32]{1,0:T(8,128)S(1)} copy(f32[384,32]{0,1:T(8,128)} %param.3) | data formatting | bytes 98304 | tf_op args[1]
  1.0 0.0 copy-done
  1.0 68.8 %shard_map.28 = f32[384,32]{1,0:T(8,128)S(1)} custom-call(bf16[384,128]{1,0:T(8,128)(2,1)S(1)} %copy-done, f32[384,32]{1,0:T(8,128)S(1)} %copy.3.start), custom_call_target="tpu_custom_call" | custom-call | tf_op jit(solution)/shard_map/pallas_call | solution.py:301
  69.8 0.7 %copy.4 = f32[384,32]{0,1:T(8,128)} copy(f32[384,32]{1,0:T(8,128)S(1)} %shard_map.28) | data formatting | bytes 98304 | tf_op jit(solution)/shard_map/pallas_call | solution.py:301
Async XLA Ops:
  0.0 1.0 %copy-start = (bf16[384,128]{1,0:T(8,128)(2,1)S(1)}, bf16[384,128]{1,0:T(8,128)(2,1)}, u32[]{:S(2)}) copy-start(bf16[384,128]{1,0:T(8,128)(2,1)} %pts.1) | copy-start | bytes 294916

commit v2 on v0

v2 whole, which is shorter than its diff:
```python
import functools
import math

import jax
import jax.numpy as jnp
from jax import lax
from jax.experimental import pallas as pl
from jax.experimental.pallas import tpu as pltpu
from jax.sharding import PartitionSpec as P

MESH = pl.DeviceIdType.MESH
HIGHEST = lax.Precision.HIGHEST
SLOPE = 8.0 / math.log(2.0)
CHUNK = 128


def layout(grp, dev):
    cores = 2
    deep = 4 if dev % 4 == 0 else dev
    return grp // cores, dev // deep, deep


def kernel(Y, X, Z, pts, start, out, units, line, it0, it1, weights, degrees, deg_out, deg_in,
           part_out, part_in, plane_buf, line_buf, usend, urecv, fsend, zsend, zrecv,
           dsend, drecv, psend, precv, gsend, grecv, lsend, lrecv):
    chips = Y * X
    panels = 2 * chips
    rows = pts.shape[0]
    width = start.shape[1]
    total = panels * Z * rows
    grp = lax.axis_index("grp")
    dev = lax.axis_index("dev")
    y, c = grp // 2, grp % 2
    z, x = dev // X, dev % X

    def ahead(k):
        a, b, d = (k // X) % Y, k % X, k // chips
        return ((y + a) % Y) * 2 + (c + d) % 2, z * X + (x + b) % X

    def behind(k):
        a, b, d = (k // X) % Y, k % X, k // chips
        return ((y + Y - a) % Y) * 2 + (c + d) % 2, z * X + (x + X - b) % X

    def below(e):
        return grp, ((z + Z - e) % Z) * X + x

    def remote(src, dst, ssem, rsem, target):
        return pltpu.make_async_remote_copy(
            src_ref=src, dst_ref=dst, send_sem=ssem, recv_sem=rsem,
            device_id=target, device_id_type=MESH,
        )

    def unit_copy(k):
        return remote(units.at[0], units.at[k], usend.at[k], urecv.at[k], behind(k))

    def unit_forward(k):
        return remote(
            units.at[k], units.at[chips + k], fsend.at[k], urecv.at[chips + k], behind(chips)
        )

    def line_copy(g, buf, e):
        return remote(buf.at[0], buf.at[e], zsend.at[g, e], zrecv.at[g, e], below(e))

    def degree_copy(k):
        return remote(deg_out.at[k], deg_in.at[k], dsend.at[k], drecv.at[k], ahead(k))

    def part_copy(g, k):
        return remote(
            part_out.at[g, k], part_in.at[g, k], psend.at[g, k], precv.at[g, k], ahead(k)
        )

    def plane_copy(g, k):
        return remote(
            plane_buf.at[g, 0], plane_buf.at[g, k], gsend.at[g, k], grecv.at[g, k], behind(k)
        )

    def plane_copies(g):
        return [plane_copy(g, k) for k in range(1, panels)]

    def line_copies(g):
        return [
            remote(line_buf.at[g, 0], line_buf.at[g, e], lsend.at[g, e], lrecv.at[g, e], below(e))
            for e in range(1, Z)
        ]

    def start_all(copies):
        for one in copies:
            one.start()

    def over(low, high, act):
        def step(k, carry):
            act(k)
            return carry
        lax.fori_loop(low, high, step, 0)

    def gram_start(g, image):
        wide = jnp.concatenate([image, jnp.zeros((128 - width, rows), jnp.float32)], axis=0)
        gram = lax.dot_general(
            image, wide, (((1,), (1,)), ((), ())), precision=HIGHEST,
            preferred_element_type=jnp.float32,
        )
        packed = gram[0:8]
        for k in range(1, width // 8):
            packed = packed + pltpu.roll(gram[8 * k:8 * k + 8], width * k, 1)
        plane_buf[g, 0] = packed
        start_all(plane_copies(g))

    def gram_middle(g):
        for one in plane_copies(g):
            one.wait_recv()
        line_buf[g, 0] = jnp.sum(plane_buf[g], axis=0)
        start_all(line_copies(g))

    def gram_end(g):
        for one in line_copies(g):
            one.wait_recv()
        packed = jnp.sum(line_buf[g], axis=0)
        lane = lax.broadcasted_iota(jnp.int32, (width, 128), 1)
        row = lax.broadcasted_iota(jnp.int32, (width, 128), 0)
        parts = [
            packed if k == 1 else pltpu.roll(packed, (width - width * k) % 128, 1)
            for k in range(width // 8)
        ]
        gram = jnp.concatenate(parts, axis=0)
        table = jnp.where((lane >= width) & (lane < 2 * width), gram, 0.0)
        table = jnp.where(lane == row, 1.0, table)
        row1 = lax.broadcasted_iota(jnp.int32, (width, 1), 0)
        for j in range(width):
            column = table[:, width + j:width + j + 1]
            inverse = 1.0 / column[j:j + 1]
            factor = jnp.where(row1 > j, column * inverse, 0.0)
            table = table - factor * table[j:j + 1]
        pivots = jnp.sum(jnp.where(lane == row + width, table, 0.0), axis=1, keepdims=True)
        return (table * lax.rsqrt(pivots))[:, :width]

    partners = [behind(k) for k in range(1, panels)] + [below(e) for e in range(1, Z)]
    barrier = pltpu.get_barrier_semaphore()
    for partner in partners:
        pl.semaphore_signal(barrier, inc=1, device_id=partner, device_id_type=MESH)

    values = pts[...].astype(jnp.float32)
    squares = jnp.sum(values * values, axis=-1, keepdims=True)
    own_units = (values * lax.rsqrt(squares + 1e-06)).astype(jnp.bfloat16)
    units[0] = own_units
    line[0] = own_units
    pl.semaphore_wait(barrier, len(partners))
    start_all([line_copy(0, line, e) for e in range(1, Z)])
    start_all([unit_copy(k) for k in range(1, chips + 1)])

    def weigh(k, e):
        theirs = units[k]
        degree = degrees[k]
        for piece in range(rows // CHUNK):
            piece = pl.ds(piece * CHUNK, CHUNK)
            cosine = lax.dot_general(
                line[e, piece], theirs, (((1,), (1,)), ((), ())),
                preferred_element_type=jnp.float32,
            )
            weight = jnp.exp2(cosine * SLOPE - SLOPE).astype(jnp.bfloat16)
            weights[k, e, piece] = weight
            weight = weight.astype(jnp.float32)
            degree = degree + jnp.sum(weight.reshape(CHUNK // 8, 8, rows), axis=0)
        degrees[k] = degree

    def near(k):
        @pl.when(k > 0)
        def _():
            unit_copy(k).wait_recv()

        @pl.when((k > 0) & (k < chips))
        def _():
            unit_forward(k).start()

        weigh(k, 0)

    def far(e):
        line_copy(0, line, e).wait_recv()
        over(0, panels, lambda k: weigh(k, e))

    def last(step):
        k = (step + 1) % panels
        weigh(k, Z - 1)
        deg_out[k] = jnp.sum(degrees[k], axis=0, keepdims=True)

        @pl.when(k > 0)
        def _():
            degree_copy(k).start()

    degrees[...] = jnp.zeros_like(degrees)
    over(0, panels, near)
    over(1, Z - 1, far)
    line_copy(0, line, Z - 1).wait_recv()
    over(0, panels, last)
    turned = start[...].T
    deg_in[0] = deg_out[0]
    over(1, panels, lambda k: degree_copy(k).wait_recv())
    scale = lax.rsqrt(jnp.sum(deg_in[...], axis=0))

    def product_of(g, buf, k):
        part = jnp.dot(buf[0], weights[k, 0], preferred_element_type=jnp.float32)
        for e in range(1, Z):
            part = part + jnp.dot(buf[e], weights[k, e], preferred_element_type=jnp.float32)
        if part.shape[0] > width:
            part = part[:width] + part[width:]
        return part

    def spread(g, buf):
        for e in range(1, Z):
            line_copy(g + 1, buf, e).wait_recv()

        def send(k):
            part_out[g, k] = product_of(g, buf, k)
            part_copy(g, k).start()

        over(1, panels, send)
        part_in[g, 0] = product_of(g, buf, 0)

    def collect(g):
        over(1, panels, lambda k: part_copy(g, k).wait_recv())
        return jnp.sum(part_in[g], axis=0)

    it0[0] = (scale * turned).astype(jnp.bfloat16)
    start_all([line_copy(1, it0, e) for e in range(1, Z)])
    spread(0, it0)
    image = scale * collect(0)

    iterate = scale * image
    high = iterate.astype(jnp.bfloat16)
    it1[0, :width] = high
    it1[0, width:] = (iterate - high.astype(jnp.float32)).astype(jnp.bfloat16)
    start_all([line_copy(2, it1, e) for e in range(1, Z)])
    gram_start(0, image)
    gram_middle(0)
    spread(1, it1)
    inverse = gram_end(0)
    product = scale * collect(1)
    image = jnp.dot(inverse, product, precision=HIGHEST, preferred_element_type=jnp.float32)

    gram_start(1, image)
    gram_middle(1)
    inverse = gram_end(1)
    vectors = jnp.dot(inverse, image, precision=HIGHEST, preferred_element_type=jnp.float32)
    out[...] = (vectors * math.sqrt(total)).T

    over(1, chips + 1, lambda k: unit_copy(k).wait_send())
    over(1, chips, lambda k: unit_forward(k).wait_send())
    over(1, panels, lambda k: degree_copy(k).wait_send())
    for g, buf in enumerate((line, it0, it1)):
        for e in range(1, Z):
            line_copy(g, buf, e).wait_send()
    for g in range(2):
        over(1, panels, lambda k: part_copy(g, k).wait_send())
        for one in plane_copies(g) + line_copies(g):
            one.wait_send()


def body(points, start_vectors):
    rows, features = points.shape
    width = start_vectors.shape[1]
    Y, X, Z = layout(lax.axis_size("grp"), lax.axis_size("dev"))
    panels = 2 * Y * X
    dma = pltpu.SemaphoreType.DMA
    shapes = [
        pltpu.VMEM((panels, rows, features), jnp.bfloat16),
        pltpu.VMEM((Z, rows, features), jnp.bfloat16),
        pltpu.VMEM((Z, width, rows), jnp.bfloat16),
        pltpu.VMEM((Z, 2 * width, rows), jnp.bfloat16),
        pltpu.VMEM((panels, Z, rows, rows), jnp.bfloat16),
        pltpu.VMEM((panels, 8, rows), jnp.float32),
        pltpu.VMEM((panels, 1, rows), jnp.float32),
        pltpu.VMEM((panels, 1, rows), jnp.float32),
        pltpu.VMEM((2, panels, width, rows), jnp.float32),
        pltpu.VMEM((2, panels, width, rows), jnp.float32),
        pltpu.VMEM((2, panels, 8, 128), jnp.float32),
        pltpu.VMEM((2, Z, 8, 128), jnp.float32),
        dma((panels,)), dma((panels,)), dma((panels,)),
        dma((3, Z)), dma((3, Z)),
        dma((panels,)), dma((panels,)),
        dma((2, panels)), dma((2, panels)),
        dma((2, panels)), dma((2, panels)),
        dma((2, Z)), dma((2, Z)),
    ]
    held = 2 * panels * rows * (features + Z * rows + 8 * width) + 2 * Z * rows * (features + 3 * width)
    return pl.pallas_call(
        functools.partial(kernel, Y, X, Z),
        out_shape=jax.ShapeDtypeStruct((rows, width), jnp.float32),
        in_specs=[pl.BlockSpec(memory_space=pltpu.VMEM)] * 2,
        out_specs=pl.BlockSpec(memory_space=pltpu.VMEM),
        scratch_shapes=shapes,
        compiler_params=pltpu.CompilerParams(
            collective_id=0, has_side_effects=True, vmem_limit_bytes=held + (5 << 20)
        ),
    )(points, start_vectors)


def solution(mesh):
    placed = (P(("grp", "dev"), None), P(("grp", "dev"), None))
    return jax.shard_map(
        body, mesh=mesh, in_specs=placed, out_specs=P(("grp", "dev"), None), check_vma=False
    )
```

time: 341 us -> 59.1 us (0.17)
  blocking collectives: 215 us -> 0 us
  waiting for transfers between devices: 62.9 us -> 0 us
  Pallas kernels: 0 us -> 57.2 us
  other arithmetic: 26.8 us -> 0 us
  matrix products: 16.3 us -> 0 us
  between operations: 13.5 us -> 0.03 us
    all_gather x2 -> x0, blocking collectives: 141 us -> none  [share_iterate(): return lax.all_gather(iterate, ('grp', 'dev'), axis=0, tiled=True)]
    psum x2 -> x0, blocking collectives: 74.1 us -> none  [orthonormal(): gram_total = lax.psum(gram_local, ('grp', 'dev'))]
    all_gather x1 -> x0, waiting for transfers between devices: 62.8 us -> none  [body(): all_units = lax.all_gather(own_units, ('grp', 'dev'), axis=0, tiled=True)]
    pallas_call x0 -> x1, Pallas kernels: none -> 57.2 us  [body(): pl.pallas_call(functools.partial(kernel, Y, X, Z), out_shape=jax.ShapeDty...]
    dot_general x6 -> x0, matrix products: 15.2 us -> none  [the longest x2 7.7 us: tile_weights(): lax.dot_general(own_units, others, (((1,), (1,)), ((), ())), preferred_el...]
    another operation x10 -> x0, other arithmetic: 13.4 us -> none  [the longest x6 7.19 us: orthonormal(): factor = jnp.linalg.cholesky(gram_total)]
    reduce_sum x2 -> x0, other arithmetic: 7.47 us -> none  [the longest x1 6.43 us: body(): degree = jnp.sum(weights, axis=1, dtype=jnp.float32)]
    broadcast_in_dim x1 -> x0, local copies, waits for them, and re-layouts: 4.4 us -> none  [weight_panel(): empty = jnp.zeros((tile_rows, count * tile_rows), jnp.bfloat16)]
  transfers between devices with their start and end apart: 1 -> 0, of which waited for: 1 -> 0; matrix products, arithmetic and copies ran while one was open for 0% -> 0% of each run, Pallas kernels for 0% -> 0%
where the time goes in v2:
time: 59.1 us; the launch traced here: 58.9 us
  Pallas kernels  57.2 us (97%)
  local copies, waits for them, and re-layouts  1.69 us (3%)
    pallas_call x1, Pallas kernels, body(): pl.pallas_call(functools.partial(kernel, Y, X, Z), out_shape=jax.ShapeDty...  57.2 us

profile of v2, /device:TPU:0, one launch (start us, length us, event | category | flops | bytes accessed | tf_op | source)
XLA Modules:
  0.0 58.9 jit_solution(11911282203256788282)
XLA Ops:
  0.0 0.0 copy-start
  0.0 1.0 %copy.3.start = f32[384,32]{1,0:T(8,128)S(1)} copy(f32[384,32]{0,1:T(8,128)} %param.3) | data formatting | bytes 98304 | tf_op args[1]
  1.0 0.0 copy-done
  1.0 57.2 %shard_map.28 = f32[384,32]{1,0:T(8,128)S(1)} custom-call(bf16[384,128]{1,0:T(8,128)(2,1)S(1)} %copy-done, f32[384,32]{1,0:T(8,128)S(1)} %copy.3.start), custom_call_target="tpu_custom_call" | custom-call | tf_op jit(solution)/shard_map/pallas_call | solution.py:284
  58.2 0.7 %copy.4 = f32[384,32]{0,1:T(8,128)} copy(f32[384,32]{1,0:T(8,128)S(1)} %shard_map.28) | data formatting | bytes 98304 | tf_op jit(solution)/shard_map/pallas_call | solution.py:284
Async XLA Ops:
  0.0 1.0 %copy-start = (bf16[384,128]{1,0:T(8,128)(2,1)S(1)}, bf16[384,128]{1,0:T(8,128)(2,1)}, u32[]{:S(2)}) copy-start(bf16[384,128]{1,0:T(8,128)(2,1)} %pts.1) | copy-start | bytes 294916
